TPU v7x, 32 devices: a whole 2x2x4 slice. The times are simulated.
32 devices in a mesh: groups: 2 (over y), ffn: 4 (over z), hid: 4 (over x, core).
Axes of the slice: x: 2, y: 2, z: 4, core: 2. Of those that a mesh axis runs over, the one named last changes fastest.
Arguments:
- act_codes: int32 [40, 8192], P(('groups', 'ffn'), 'hid'), parts along dimension 0, may hold values from -127 to 127
- act_exps: int32 [40, 64], P(('groups', 'ffn'), 'hid'), parts along dimension 0, may hold values from -10 to -7
- gate_codes: bfloat16 [8192, 26624], P('hid', 'ffn'), may hold values from -8 to 7, as said below
- up_codes: bfloat16 [8192, 26624], P('hid', 'ffn'), may hold values from -8 to 7, as said below
- down_codes: bfloat16 [26624, 8192], P('ffn', 'hid'), may hold values from -8 to 7, as said below
- gate_scale: float32 [26624], P('ffn'), may hold values from 0.004 to 0.016
- up_scale: float32 [26624], P('ffn'), may hold values from 0.004 to 0.016
- down_scale: float32 [8192], P('hid'), may hold values from 0.0015 to 0.006
Outputs:
- layer_out: bfloat16 [40, 8192], P(('groups', 'ffn'), 'hid'), parts along dimension 0
There are 2 independent parts, one for each index of `groups`. A program takes and returns all parts, laid end to end along the dimension named above; an argument that names none is the same for every part. Nothing has to cross between parts.
Inputs may be any that keep to these rules, and one draw needn't show every extreme that they name: `gate_codes`: integer levels. `up_codes`: integer levels. `down_codes`: integer levels.
All inputs are finite; a program needn't handle non-finite values.
Results may differ from a plain program's by a relative error of at most 0.0058.
Values may be sent and summed in bfloat16 or wider, within the bound.
A program may use at most 192 MiB of HBM per device.

v0:
```python
import jax
import jax.numpy as jnp
import numpy as np
from jax import lax
from jax.sharding import PartitionSpec as P


def field_product(first, second):
    return (
        (first[0] * second[0] + 2 * first[1] * second[1]) % 5,
        (first[0] * second[1] + first[1] * second[0]) % 5,
    )


def paley_table():
    elements = [(alpha, beta) for alpha in range(5) for beta in range(5)]
    squares = set()
    for item in elements:
        if item != (0, 0):
            squares.add(field_product(item, item))
    jacobi = np.zeros((25, 25))
    for left in range(25):
        for right in range(25):
            diff = (
                (elements[left][0] - elements[right][0]) % 5,
                (elements[left][1] - elements[right][1]) % 5,
            )
            if diff == (0, 0):
                jacobi[left, right] = 0.0
            elif diff in squares:
                jacobi[left, right] = 1.0
            else:
                jacobi[left, right] = -1.0
    conference = np.zeros((26, 26))
    conference[0, 1:] = 1.0
    conference[1:, 0] = 1.0
    conference[1:, 1:] = jacobi
    return np.kron(conference, np.array([[1.0, -1.0], [-1.0, -1.0]])) + np.kron(
        np.eye(26), np.array([[1.0, 1.0], [1.0, -1.0]])
    )


def sylvester_table(order):
    table = np.ones((1, 1))
    while table.shape[0] < order:
        table = np.kron(table, np.array([[1.0, 1.0], [1.0, -1.0]]))
    return table


def activate(sums, gate_scale, up_scale, width):
    gate = sums[:, :width] * gate_scale
    up_val = sums[:, width:] * up_scale
    return (jax.nn.silu(gate) * up_val).astype(jnp.bfloat16)


def on_device(
    act_codes, act_exps, gate_codes, up_codes, down_codes, gate_scale, up_scale, down_scale
):
    row_count, col_count = act_codes.shape
    blocks = act_exps.shape[1]
    scales = jnp.exp2(act_exps.astype(jnp.float32))
    features = (
        (
            act_codes.reshape(row_count, blocks, col_count // blocks).astype(jnp.float32)
            * scales[:, :, None]
        )
        .reshape(row_count, col_count)
        .astype(jnp.bfloat16)
    )
    width = gate_codes.shape[1]
    piece = lax.all_gather(features, "ffn", axis=0, tiled=True)
    gate_part = jnp.dot(piece, gate_codes, preferred_element_type=jnp.float32)
    up_part = jnp.dot(piece, up_codes, preferred_element_type=jnp.float32)
    partial_sums = jnp.concatenate([gate_part, up_part], axis=1)
    summed = lax.psum(partial_sums, "hid")
    hidden = activate(summed, gate_scale, up_scale, width)
    parts = lax.axis_size("ffn")
    tokens = hidden.shape[0]
    per_dev = tokens // parts
    local = width // 52
    small_table = jnp.asarray(paley_table(), dtype=jnp.bfloat16)
    outer_table = jnp.asarray(sylvester_table(parts), dtype=jnp.float32)
    inner_table = jnp.asarray(sylvester_table(local), dtype=jnp.float32)
    norm_factor = 1.0 / np.sqrt(parts * width)
    grouped = hidden.reshape(parts, per_dev, width)
    block = lax.all_to_all(grouped, "ffn", split_axis=0, concat_axis=0, tiled=True)
    items = block.shape[1]
    cube = block.reshape(parts, items, local, 52)
    mixed = jnp.einsum("snli,ik->snlk", cube, small_table, preferred_element_type=jnp.float32)
    across = jnp.einsum("snlk,sS->Snlk", mixed, outer_table, precision=lax.Precision.HIGHEST)
    turned = jnp.einsum("Snlk,lL->SnLk", across, inner_table, precision=lax.Precision.HIGHEST)
    rotated = (turned * norm_factor).reshape(parts, items, width).astype(jnp.bfloat16)
    returned = lax.all_to_all(rotated, "ffn", split_axis=0, concat_axis=0, tiled=True)
    rotated_rows = returned.reshape(tokens, width)
    total = lax.psum_scatter(
        jnp.dot(rotated_rows, down_codes, preferred_element_type=jnp.float32),
        "ffn",
        scatter_dimension=0,
        tiled=True,
    )
    return (total * down_scale).astype(jnp.bfloat16)


def solution(mesh):
    in_specs = (
        P(("groups", "ffn"), "hid"),
        P(("groups", "ffn"), "hid"),
        P("hid", "ffn"),
        P("hid", "ffn"),
        P("ffn", "hid"),
        P("ffn"),
        P("ffn"),
        P("hid"),
    )
    out_specs = P(("groups", "ffn"), "hid")
    return jax.shard_map(
        on_device, mesh=mesh, in_specs=in_specs, out_specs=out_specs, check_vma=False
    )
```

profile of v0, /device:TPU:0, one launch (start us, length us, event | category | flops | bytes accessed | tf_op | source)
XLA Modules:
  0.0 163.4 jit_solution(18287076763522463819)
XLA Ops:
  6.5 0.7 multiply_exponential_fusion
  7.3 0.9 fusion.10
  8.2 15.1 %all-gather = bf16[4,5,2048]{2,1,0:T(8,128)(2,1)S(1)} all-gather(bf16[1,5,2048]{2,1,0:T(8,128)(2,1)S(1)} %fusion.10), channel_id=1, replica_groups=mesh['groups'=2,'ffn'=4,'hid'=4] {'ffn'}, dimensions={0}, use_global_device_ids=true | all-gather | bytes 102400 | tf_op jit(solution)/shard_map/all_gather | solution.py:71
  23.3 10.6 %fusion.11 = f32[20,6656]{1,0:T(8,128)S(1)} fusion(bf16[20,2048]{1,0:T(8,128)(2,1)S(1)} %reshape.22, bf16[2048,6656]{1,0:T(8,128)(2,1)} %param.13), kind=kOutput, calls=%fused_computation.18 | convolution fusion | flops 545259520 | bytes 27877376 | tf_op jit(solution)/shard_map/dot_general | solution.py:72
  34.0 10.7 %fusion.12 = f32[20,6656]{1,0:T(8,128)S(1)} fusion(bf16[20,2048]{1,0:T(8,128)(2,1)S(1)} %reshape.22, bf16[2048,6656]{1,0:T(8,128)(2,1)} %param.14), kind=kOutput, calls=%fused_computation.19 | convolution fusion | flops 545259520 | bytes 27877376 | tf_op jit(solution)/shard_map/dot_general | solution.py:73
  44.7 1.1 pad_maximum_fusion
  45.8 40.0 %all-reduce.4.cloned.1.call-done = f32[20,13312]{1,0:T(8,128)} async-done(((f32[20,13312]{1,0:T(8,128)}), f32[20,13312]{1,0:T(8,128)}) %all-reduce.4.cloned.1.call-update) | async-done | bytes 1064976 | tf_op jit(solution)/shard_map/psum | solution.py:75
  85.8 1.5 fusion.4
  87.3 0.1 reshape.18
  87.4 16.8 %all_to_all.10 = bf16[4,5,6656]{2,1,0:T(8,128)(2,1)S(1)} all-to-all(bf16[4,5,6656]{2,1,0:T(8,128)(2,1)S(1)} %reshape.18), channel_id=1, replica_groups=mesh['groups'=2,'ffn'=4,'hid'=4] {'ffn'}, dimensions={0} | all-to-all | bytes 532480 | tf_op jit(solution)/shard_map/all_to_all | solution.py:86
  104.2 2.0 %reshape.26 = bf16[4,5,128,52]{3,2,1,0:T(8,128)(2,1)S(1)} reshape(bf16[4,5,6656]{2,1,0:T(8,128)(2,1)S(1)} %all_to_all.10) | data formatting | bytes 532480 | tf_op jit(solution)/shard_map/reshape | solution.py:88
  106.2 0.5 fusion.13
  106.7 1.0 fusion.6
  107.7 0.6 fusion.2
  108.3 0.4 copy.27
  108.7 1.7 %reshape.27 = bf16[4,5,6656]{2,1,0:T(8,128)(2,1)S(1)} reshape(bf16[4,5,128,52]{3,2,1,0:T(8,128)(2,1)S(1)} %copy.27) | data formatting | bytes 532480 | tf_op jit(solution)/shard_map/convert_element_type | solution.py:92
  110.4 14.2 %all_to_all.11 = bf16[4,5,6656]{2,1,0:T(8,128)(2,1)S(1)} all-to-all(bf16[4,5,6656]{2,1,0:T(8,128)(2,1)S(1)} %reshape.27), channel_id=1, replica_groups=mesh['groups'=2,'ffn'=4,'hid'=4] {'ffn'}, dimensions={0} | all-to-all | bytes 532480 | tf_op jit(solution)/shard_map/all_to_all | solution.py:93
  124.7 10.6 %fusion.14 = f32[20,2048]{1,0:T(8,128)S(1)} fusion(bf16[20,6656]{1,0:T(8,128)(2,1)S(1)} %reshape.20, bf16[6656,2048]{1,0:T(8,128)(2,1)} %param.15), kind=kOutput, calls=%fused_computation.21 | convolution fusion | flops 545259520 | bytes 27693056 | tf_op jit(solution)/shard_map/dot_general | solution.py:96
  135.3 14.8 %fusion = f32[8,2048]{1,0:T(8,128)S(1)} fusion(f32[20,2048]{1,0:T(8,128)S(1)} %fusion.14), kind=kCustom, calls=%all-reduce-scatter | all-reduce-scatter fusion | flops 65537 | bytes 229888
  150.2 1.3 collective-permute-start
  151.5 2.8 %collective-permute-start.1 = (f32[1,2048]{1,0:T(1,128)S(1)}, f32[1,2048]{1,0:T(1,128)S(1)}, u32[]{:S(2)}, u32[]{:S(2)}) collective-permute-start(f32[1,2048]{1,0:T(1,128)S(1)} %slice.10), channel_id=1, source_target_pairs={{0,8},{4,12},{1,9},{5,13},{2,10},{6,14},{3,11},{7,15},{16,24},{20,... | collective-permute-start | bytes 24584
  154.2 0.6 dynamic-slice.4
  155.6 0.3 concatenate.4
  155.9 0.6 fusion.9
  (22 shorter events, 0.4 us)
Async XLA Ops:
  6.5 79.3 %all-reduce.4.cloned.1.call-start = ((), (), s32[]{:S(2)}) async-start(), calls=%async_computation.2 | async-start | bytes 2555904 | tf_op jit(solution)/shard_map/psum | solution.py:75
  23.3 62.5 %copy-start.1 = (f32[6656]{0:T(1024)S(1)}, f32[6656]{0:T(1024)}, u32[]{:S(2)}) copy-start(f32[6656]{0:T(1024)} %param.17) | copy-start | bytes 79876
  23.3 62.5 %copy-start.2 = (f32[6656]{0:T(1024)S(1)}, f32[6656]{0:T(1024)}, u32[]{:S(2)}) copy-start(f32[6656]{0:T(1024)} %param.16) | copy-start | bytes 79876
  33.9 72.2 %copy-start.3 = (bf16[52,52,1,1]{0,1,3,2:T(8,128)(2,1)S(1)}, bf16[52,52,1,1]{0,1,3,2:T(8,128)(2,1)}, u32[]{:S(2)}) copy-start(bf16[52,52,1,1]{0,1,3,2:T(8,128)(2,1)} %constant.23) | copy-start | bytes 16228
  33.9 72.7 %copy-start.5 = (f32[4,4,1,1]{0,1,3,2:T(4,128)S(1)}, f32[4,4,1,1]{0,1,3,2:T(4,128)}, u32[]{:S(2)}) copy-start(f32[4,4,1,1]{0,1,3,2:T(4,128)} %constant.22) | copy-start | bytes 196
  34.0 73.7 %copy-start = (f32[128,128,1,1]{1,0,3,2:T(8,128)S(1)}, f32[128,128,1,1]{1,0,3,2:T(8,128)}, u32[]{:S(2)}) copy-start(f32[128,128,1,1]{1,0,3,2:T(8,128)} %constant.24) | copy-start | bytes 196612
  44.6 109.6 %copy-start.6 = (u32[32]{0:T(128)S(1)}, u32[32]{0:T(128)}, u32[]{:S(2)}) copy-start(u32[32]{0:T(128)} %constant.20) | copy-start | bytes 388
  44.6 111.2 %copy-start.4 = (f32[2048]{0:T(1024)S(1)}, f32[2048]{0:T(1024)}, u32[]{:S(2)}) copy-start(f32[2048]{0:T(1024)} %param.18) | copy-start | bytes 24580
  150.2 5.4 %collective-permute-start = (f32[8,2048]{1,0:T(8,128)S(1)}, f32[8,2048]{1,0:T(8,128)S(1)}, u32[]{:S(2)}, u32[]{:S(2)}) collective-permute-start(f32[8,2048]{1,0:T(8,128)S(1)} %fusion), channel_id=1, source_target_pairs={{0,4},{4,8},{8,12},{1,5},{5,9},{9,13},{2,6},{6,10},{10,14},{3,7},{... | collective-permute-start | bytes 196616
  151.5 4.1 %collective-permute-start.1 = (f32[1,2048]{1,0:T(1,128)S(1)}, f32[1,2048]{1,0:T(1,128)S(1)}, u32[]{:S(2)}, u32[]{:S(2)}) collective-permute-start(f32[1,2048]{1,0:T(1,128)S(1)} %slice.10), channel_id=1, source_target_pairs={{0,8},{4,12},{1,9},{5,13},{2,10},{6,14},{3,11},{7,15},{16,24},{20,... | collective-permute-start | bytes 24584
Sparse Core Ops, SparseCore 0:
  45.9 39.8 all-reduce.3
where the time goes:
time: 164 us; the launch traced here: 163 us
  blocking collectives  60.8 us (37%)
  waiting for transfers between devices  40.1 us (24%)
  matrix products  34 us (21%)
  between operations  14.2 us (9%)
  local copies, waits for them, and re-layouts  5.3 us (3%)
  other arithmetic  4.8 us (3%)
  starting transfers between devices  4.05 us (2%)
    psum x1, waiting for transfers between devices, on_device(): summed = lax.psum(partial_sums, 'hid')  40 us
    all_to_all x1, blocking collectives, on_device(): lax.all_to_all(grouped, 'ffn', split_axis=0, concat_axis=0, tiled=True)  16.8 us
    all_gather x1, blocking collectives, on_device(): piece = lax.all_gather(features, 'ffn', axis=0, tiled=True)  15.1 us
    unnamed x1, blocking collectives  14.8 us
    all_to_all x1, blocking collectives, on_device(): lax.all_to_all(rotated, 'ffn', split_axis=0, concat_axis=0, tiled=True)  14.2 us
    dot_general x1, matrix products, on_device(): up_part = jnp.dot(piece, up_codes, preferred_element_type=jnp.float32)  10.7 us
    dot_general x1, matrix products, on_device(): jnp.dot(rotated_rows, down_codes, preferred_element_type=jnp.float32)  10.6 us
    dot_general x1, matrix products, on_device(): gate_part = jnp.dot(piece, gate_codes, preferred_element_type=jnp.float32)  10.6 us
  transfers between devices with their start and end apart: 3, of which 2 were waited for; matrix products, arithmetic and copies ran while one was open for 0% of the time, Pallas kernels for 0%

commit v1 on v0

--- a/solution.py
+++ b/solution.py
@@ -1,8 +1,14 @@
+import functools
+
 import jax
 import jax.numpy as jnp
 import numpy as np
 from jax import lax
+from jax.experimental import pallas as pl
+from jax.experimental.pallas import tpu as pltpu
 from jax.sharding import PartitionSpec as P
+
+MESH = pl.DeviceIdType.MESH
 
 
 def field_product(first, second):
@@ -101,6 +107,326 @@
     return (total * down_scale).astype(jnp.bfloat16)
 
 
+LANES = 128
+ORDER = 52
+SPLIT = 4
+TILE_ROWS = 512
+RING = 10
+PAD = 24
+FULL = 32
+
+
+def flip(index, mask):
+    if mask == 1:
+        return index + 1 - 2 * (index % 2)
+    if mask == 2:
+        return (index + 2) % 4
+    if mask == 3:
+        return 3 - index
+    return index
+
+
+def sign_of(first, second):
+    low = (first % 2) * (second % 2)
+    high = (first // 2) * (second // 2)
+    odd = (low + high) % 2
+    return jnp.asarray(1 - 2 * odd, jnp.int32).astype(jnp.float32)
+
+
+def cut_chunk(blocks):
+    cuts = []
+    while blocks > 5:
+        cuts.append(4)
+        blocks -= 4
+    if blocks > 2:
+        cuts += [blocks - 2, 2]
+    else:
+        cuts.append(blocks)
+    return cuts
+
+
+def layer_kernel(plan, *refs):
+    rows, depth, width, feats, norm = plan
+    chunk = width // SPLIT
+    cuts = [blocks * LANES for blocks in cut_chunk(chunk // LANES)]
+    starts = [sum(cuts[:index]) for index in range(len(cuts))]
+    count = len(cuts)
+    tokens = rows * SPLIT
+    blocks = depth // LANES
+    down_tiles = width // TILE_ROWS
+    refs = list(refs)
+    (codes, exps, gate_hbm, up_hbm, down_hbm, gscale, uscale, dscale, table_hbm, out) = refs[:10]
+    (ring, table, down, gs, us, fold, xrecv, xfull, xmat, zsum, zall, rot, part, obuf, orecv) = refs[10:25]
+    psend = refs[25 : 25 + count]
+    precv = refs[25 + count : 25 + 2 * count]
+    hall = refs[25 + 2 * count : 25 + 3 * count]
+    (ring_sem, table_sem, down_sem, scale_sem, xs, xr, ps, pr, hs, hr, zs, zr, os, orr) = refs[25 + 3 * count :]
+    me_f = lax.axis_index("ffn")
+    me_h = lax.axis_index("hid")
+
+    masks = (2, 3, 1, 0)
+    units = []
+    for sub in range(count):
+        for mask in masks:
+            units.append((sub, mask, 0))
+            units.append((sub, mask, 1))
+
+    def unit_copy(index):
+        sub, mask, which = units[index]
+        source = up_hbm if which else gate_hbm
+        slot = index % RING
+        at = pl.multiple_of(flip(me_h, mask) * chunk + starts[sub], LANES)
+        return pltpu.make_async_copy(
+            source.at[:, pl.ds(at, cuts[sub])],
+            ring.at[slot, :, pl.ds(0, cuts[sub])],
+            ring_sem.at[slot],
+        )
+
+    def down_copy(index):
+        piece = pl.ds(index * TILE_ROWS, TILE_ROWS)
+        return pltpu.make_async_copy(down_hbm.at[piece, :], down.at[piece, :], down_sem.at[index])
+
+    def table_copy(sub):
+        piece = pl.ds(starts[sub], cuts[sub])
+        return pltpu.make_async_copy(table_hbm.at[piece, :], table.at[piece, :], table_sem.at[sub])
+
+    def scale_copy(which):
+        source, target = ((gscale, gs), (uscale, us))[which]
+        at = pl.multiple_of(me_h * chunk, LANES)
+        return pltpu.make_async_copy(source.at[:, pl.ds(at, chunk)], target, scale_sem.at[which])
+
+    for which in range(2):
+        scale_copy(which).start()
+    for index in range(min(RING, len(units))):
+        unit_copy(index).start()
+    for sub in range(count):
+        table_copy(sub).start()
+
+    barrier = pltpu.get_barrier_semaphore()
+    for mask in (1, 2, 3):
+        pl.semaphore_signal(barrier, inc=1, device_id={"ffn": flip(me_f, mask)}, device_id_type=MESH)
+        pl.semaphore_signal(barrier, inc=1, device_id={"hid": flip(me_h, mask)}, device_id_type=MESH)
+
+    powers = lax.shift_left(jnp.ones_like(exps[...]), exps[...] + 10).astype(jnp.float32) * (2.0**-10)
+    for block in range(blocks):
+        at = block * LANES
+        scale = powers[:, at // feats : at // feats + 1]
+        fold[0, pl.ds(block * rows, rows), :] = codes[:, pl.ds(at, LANES)].astype(jnp.float32) * scale
+    xrecv[0] = fold[0].astype(jnp.bfloat16)
+    pl.semaphore_wait(barrier, 6)
+
+    def feat_copy(mask):
+        return pltpu.make_async_remote_copy(
+            src_ref=xrecv.at[0], dst_ref=xrecv.at[mask], send_sem=xs.at[mask - 1], recv_sem=xr.at[mask - 1],
+            device_id={"ffn": flip(me_f, mask)}, device_id_type=MESH,
+        )
+
+    for mask in (3, 2, 1):
+        feat_copy(mask).start()
+    xfull[...] = jnp.zeros_like(xfull)
+    for mask in (1, 2, 3):
+        feat_copy(mask).wait_recv()
+    for mask in range(4):
+        fold[flip(me_f, mask)] = xrecv[mask].astype(jnp.float32)
+    for owner in range(SPLIT):
+        for block in range(blocks):
+            xfull[pl.ds(owner * rows, rows), pl.ds(block * LANES, LANES)] = fold[owner, pl.ds(block * rows, rows), :]
+    xmat[...] = xfull[...].astype(jnp.bfloat16)
+
+    def part_copy(sub, mask):
+        return pltpu.make_async_remote_copy(
+            src_ref=psend[sub].at[mask], dst_ref=precv[sub].at[mask - 1],
+            send_sem=ps.at[sub * 3 + mask - 1], recv_sem=pr.at[sub * 3 + mask - 1],
+            device_id={"hid": flip(me_h, mask)}, device_id_type=MESH,
+        )
+
+    def hidden_copy(sub, mask):
+        return pltpu.make_async_remote_copy(
+            src_ref=hall[sub].at[0], dst_ref=hall[sub].at[mask],
+            send_sem=hs.at[sub * 3 + mask - 1], recv_sem=hr.at[sub * 3 + mask - 1],
+            device_id={"ffn": flip(me_f, mask)}, device_id_type=MESH,
+        )
+
+    def z_copy(mask):
+        return pltpu.make_async_remote_copy(
+            src_ref=zall.at[0], dst_ref=zall.at[mask], send_sem=zs.at[mask - 1], recv_sem=zr.at[mask - 1],
+            device_id={"hid": flip(me_h, mask)}, device_id_type=MESH,
+        )
+
+    def out_copy(mask):
+        return pltpu.make_async_remote_copy(
+            src_ref=obuf.at[flip(me_f, mask)], dst_ref=orecv.at[mask - 1],
+            send_sem=os.at[mask - 1], recv_sem=orr.at[mask - 1],
+            device_id={"ffn": flip(me_f, mask)}, device_id_type=MESH,
+        )
+
+    def finish_hidden(sub):
+        if sub == 0:
+            for which in range(2):
+                scale_copy(which).wait()
+        for mask in (1, 2, 3):
+            part_copy(sub, mask).wait_recv()
+        piece = pl.ds(starts[sub], cuts[sub])
+        sums = []
+        for which in range(2):
+            total = psend[sub][0, which]
+            for mask in (1, 2, 3):
+                total = total + precv[sub][mask - 1, which]
+            sums.append(total)
+        gate = sums[0] * gs[:, piece]
+        value = gate / (1.0 + jnp.exp(-gate)) * (sums[1] * us[:, piece])
+        padded = jnp.concatenate([value, jnp.zeros((FULL - PAD, cuts[sub]), jnp.float32)], axis=0)
+        hall[sub][0] = padded.astype(jnp.bfloat16)
+        for mask in (3, 2, 1):
+            hidden_copy(sub, mask).start()
+
+    def mix(sub):
+        table_copy(sub).wait()
+        total = hall[sub][0].astype(jnp.float32) * sign_of(me_f, me_f)
+        for mask in (1, 2, 3):
+            hidden_copy(sub, mask).wait_recv()
+            total = total + hall[sub][mask].astype(jnp.float32) * sign_of(flip(me_f, mask), me_f)
+        total = total[:PAD]
+        high = total.astype(jnp.bfloat16).astype(jnp.float32)
+        both = jnp.concatenate([high, total - high], axis=0).astype(jnp.bfloat16)
+        mixed = jnp.dot(both, table[pl.ds(starts[sub], cuts[sub]), :], preferred_element_type=jnp.float32)
+        mixed = mixed[:PAD] + mixed[PAD:]
+        if sub == 0:
+            zsum[...] = mixed
+        else:
+            zsum[...] += mixed
+
+    down_next = 0
+    for index, (sub, mask, which) in enumerate(units):
+        unit_copy(index).wait()
+        slot = index % RING
+        value = jnp.dot(xmat[...], ring[slot, :, pl.ds(0, cuts[sub])], preferred_element_type=jnp.float32)
+        psend[sub][mask, which] = value[:PAD]
+        if index + RING < len(units):
+            unit_copy(index + RING).start()
+        elif down_next < down_tiles:
+            down_copy(down_next).start()
+            down_next += 1
+        if which == 1:
+            if mask != 0:
+                part_copy(sub, mask).start()
+            if mask == 3 and sub >= 1:
+                finish_hidden(sub - 1)
+            if mask == 0 and sub >= 1:
+                mix(sub - 1)
+    while down_next < down_tiles:
+        down_copy(down_next).start()
+        down_next += 1
+    finish_hidden(count - 1)
+    mix(count - 1)
+
+    padded = jnp.concatenate([zsum[...], jnp.zeros((FULL - PAD, chunk), jnp.float32)], axis=0)
+    zall[0] = padded.astype(jnp.bfloat16)
+    for mask in (3, 2, 1):
+        z_copy(mask).start()
+    for index in range(down_tiles):
+        down_copy(index).wait()
+    for mask in (1, 2, 3):
+        z_copy(mask).wait_recv()
+    for target in range(SPLIT):
+        total = zall[0].astype(jnp.float32) * (sign_of(me_h, target) * norm)
+        for mask in (1, 2, 3):
+            total = total + zall[mask].astype(jnp.float32) * (sign_of(flip(me_h, mask), target) * norm)
+        rot[target] = total.astype(jnp.bfloat16)
+
+    @pl.loop(0, depth // 512)
+    def _(tile):
+        at = pl.ds(pl.multiple_of(tile * 512, 512), 512)
+        total = jnp.zeros((FULL, 512), jnp.float32)
+        for target in range(SPLIT):
+            total = total + jnp.dot(
+                rot[target], down[pl.ds(target * chunk, chunk), at], preferred_element_type=jnp.float32
+            )
+        part[:, at] = total
+
+    for owner in range(SPLIT):
+        for block in range(blocks):
+            fold[owner, pl.ds(block * rows, rows), :] = part[pl.ds(owner * rows, rows), pl.ds(block * LANES, LANES)]
+    obuf[...] = fold[...].astype(jnp.bfloat16)
+    for mask in (3, 2, 1):
+        out_copy(mask).start()
+    total = fold[me_f]
+    for mask in (1, 2, 3):
+        out_copy(mask).wait_recv()
+        total = total + orecv[mask - 1].astype(jnp.float32)
+    fold[0] = total
+    for block in range(blocks):
+        at = pl.ds(block * LANES, LANES)
+        out[:, at] = (fold[0, pl.ds(block * rows, rows), :] * dscale[:, at]).astype(jnp.bfloat16)
+
+    for mask in (1, 2, 3):
+        feat_copy(mask).wait_send()
+        z_copy(mask).wait_send()
+        out_copy(mask).wait_send()
+        for sub in range(count):
+            part_copy(sub, mask).wait_send()
+            hidden_copy(sub, mask).wait_send()
+
+
+def fused_on_device(
+    act_codes, act_exps, gate_codes, up_codes, down_codes, gate_scale, up_scale, down_scale
+):
+    rows, depth = act_codes.shape
+    width = gate_codes.shape[1]
+    chunk = width // SPLIT
+    feats = depth // act_exps.shape[1]
+    cuts = [blocks * LANES for blocks in cut_chunk(chunk // LANES)]
+    count = len(cuts)
+    norm = float(1.0 / np.sqrt(width * lax.axis_size("ffn")))
+    table = jnp.asarray(
+        np.kron(sylvester_table(chunk // ORDER), paley_table()).astype(np.float32), dtype=jnp.bfloat16
+    )
+    folded = rows * (depth // LANES)
+    vmem = pl.BlockSpec(memory_space=pltpu.VMEM)
+    hbm = pl.BlockSpec(memory_space=pl.ANY)
+    f32, bf16 = jnp.float32, jnp.bfloat16
+    scratch = [
+        pltpu.VMEM((RING, depth, max(cuts)), bf16),
+        pltpu.VMEM((chunk, chunk), bf16),
+        pltpu.VMEM((width, depth), bf16),
+        pltpu.VMEM((1, chunk), f32),
+        pltpu.VMEM((1, chunk), f32),
+        pltpu.VMEM((SPLIT, folded, LANES), f32),
+        pltpu.VMEM((SPLIT, folded, LANES), bf16),
+        pltpu.VMEM((FULL, depth), f32),
+        pltpu.VMEM((FULL, depth), bf16),
+        pltpu.VMEM((PAD, chunk), f32),
+        pltpu.VMEM((SPLIT, FULL, chunk), bf16),
+        pltpu.VMEM((SPLIT, FULL, chunk), bf16),
+        pltpu.VMEM((FULL, depth), f32),
+        pltpu.VMEM((SPLIT, folded, LANES), bf16),
+        pltpu.VMEM((SPLIT - 1, folded, LANES), bf16),
+    ]
+    scratch += [pltpu.VMEM((SPLIT, 2, PAD, cut), f32) for cut in cuts]
+    scratch += [pltpu.VMEM((SPLIT - 1, 2, PAD, cut), f32) for cut in cuts]
+    scratch += [pltpu.VMEM((SPLIT, FULL, cut), bf16) for cut in cuts]
+    dma = pltpu.SemaphoreType.DMA
+    scratch += [dma((RING,)), dma((count,)), dma((width // TILE_ROWS,)), dma((2,)), dma((3,)), dma((3,))]
+    scratch += [dma((3 * count,)) for _ in range(4)]
+    scratch += [dma((3,)) for _ in range(4)]
+    return pl.pallas_call(
+        functools.partial(layer_kernel, (rows, depth, width, feats, norm)),
+        out_shape=jax.ShapeDtypeStruct((rows, depth), bf16),
+        in_specs=[vmem, vmem, hbm, hbm, hbm, hbm, hbm, vmem, hbm],
+        out_specs=vmem,
+        scratch_shapes=scratch,
+        compiler_params=pltpu.CompilerParams(
+            collective_id=0, has_side_effects=True, vmem_limit_bytes=62 * 2**20
+        ),
+        cost_estimate=pl.CostEstimate(
+            flops=6 * rows * SPLIT * depth * width, bytes_accessed=6 * depth * width, transcendentals=0
+        ),
+    )(
+        act_codes, act_exps, gate_codes, up_codes, down_codes,
+        gate_scale.reshape(1, width), up_scale.reshape(1, width), down_scale.reshape(1, depth), table,
+    )
+
+
 def solution(mesh):
     in_specs = (
         P(("groups", "ffn"), "hid"),
@@ -113,6 +439,7 @@
         P("hid"),
     )
     out_specs = P(("groups", "ffn"), "hid")
+    square = mesh.shape["ffn"] == SPLIT and mesh.shape["hid"] == SPLIT
     return jax.shard_map(
-        on_device, mesh=mesh, in_specs=in_specs, out_specs=out_specs, check_vma=False
-    )
+        fused_on_device if square else on_device, mesh=mesh, in_specs=in_specs, out_specs=out_specs, check_vma=False
+    )

time: 164 us -> 57 us (0.35)
  blocking collectives: 60.8 us -> 0 us
  Pallas kernels: 0 us -> 52.5 us
  waiting for transfers between devices: 40.1 us -> 0 us
  matrix products: 34 us -> 0 us
  between operations: 14.2 us -> 0.01 us
  other arithmetic: 4.8 us -> 0 us
  starting transfers between devices: 4.05 us -> 0 us
    pallas_call x0 -> x1, Pallas kernels: none -> 52.5 us  [fused_on_device(): pl.pallas_call(functools.partial(layer_kernel, (rows, depth, width, feats...]
    psum x1 -> x0, waiting for transfers between devices: 40 us -> none  [on_device(): summed = lax.psum(partial_sums, 'hid')]
    dot_general x6 -> x0, matrix products: 34 us -> none  [the longest x1 10.7 us: on_device(): up_part = jnp.dot(piece, up_codes, preferred_element_type=jnp.float32)]
    all_to_all x2 -> x0, blocking collectives: 30.9 us -> none  [the longest x1 16.8 us: on_device(): lax.all_to_all(grouped, 'ffn', split_axis=0, concat_axis=0, tiled=True)]
    all_gather x1 -> x0, blocking collectives: 15.1 us -> none  [on_device(): piece = lax.all_gather(features, 'ffn', axis=0, tiled=True)]
    unnamed x1 -> x0, blocking collectives: 14.8 us -> none
    unnamed x2 -> x0, starting transfers between devices: 4.05 us -> none
    convert_element_type x2 -> x0, other arithmetic: 2.1 us -> none  [the longest x1 1.47 us: activate(): return (jax.nn.silu(gate) * up_val).astype(jnp.bfloat16)]
  transfers between devices with their start and end apart: 3 -> 0, of which waited for: 2 -> 0; matrix products, arithmetic and copies ran while one was open for 0% -> 0% of each run, Pallas kernels for 0% -> 0%
where the time goes in v1:
time: 57 us; the launch traced here: 56.6 us
  Pallas kernels  52.5 us (92%)
  local copies, waits for them, and re-layouts  4.11 us (7%)
    pallas_call x1, Pallas kernels, fused_on_device(): pl.pallas_call(functools.partial(layer_kernel, (rows, depth, width, feats...  52.5 us
    unnamed x1, local copies, waits for them, and re-layouts  1.38 us
    reshape x1, local copies, waits for them, and re-layouts, fused_on_device(): gate_scale.reshape(1, width)  1.37 us
    reshape x1, local copies, waits for them, and re-layouts, fused_on_device(): up_scale.reshape(1, width)  1.36 us

profile of v1, /device:TPU:0, one launch (start us, length us, event | category | flops | bytes accessed | tf_op | source)
XLA Modules:
  0.0 56.6 jit_solution(3166342578117229694)
XLA Ops:
  0.0 1.4 %reshape.9.refs_5_ = f32[1,6656]{1,0:T(1,128)} reshape(f32[6656]{0:T(1024)} %param.14) | data formatting | bytes 53248 | tf_op jit(solution)/shard_map/reshape | solution.py:426
  1.4 1.4 %reshape.10.refs_6_ = f32[1,6656]{1,0:T(1,128)} reshape(f32[6656]{0:T(1024)} %param.15) | data formatting | bytes 53248 | tf_op jit(solution)/shard_map/reshape | solution.py:426
  2.7 52.5 %shard_map.91 = bf16[5,2048]{1,0:T(8,128)(2,1)} custom-call(s32[5,2048]{1,0:T(8,128)} %refs_0_.1, s32[5,16]{1,0:T(8,128)} %refs_1_.1, bf16[2048,6656]{1,0:T(8,128)(2,1)} %refs_2_.1, bf16[2048,6656]{1,0:T(8,128)(2,1)} %refs_3_.1, bf16[6656,2048]{1,0:T(8,128)(2,1)} %refs_4_.1, f32[1,6656]{1,0:T(1,128)} %reshape.9.refs_5_, f32[1,6656]{1,0:T(1,128)} %reshape.10.refs_6_, ...), custom_call_target="tpu_custom_call" | custom-call | flops 1635778560 | bytes 81788928 | tf_op jit(solution)/shard_map/pallas_call | solution.py:412
  55.2 1.4 %copy.11 = bf16[5,2048]{1,0:T(8,128)(2,1)} copy(bf16[5,2048]{1,0:T(8,128)(2,1)} %shard_map.91) | data formatting | bytes 40960

commit v2 on v1

v2 whole, which is shorter than its diff:
```python
import functools

import jax
import jax.numpy as jnp
import numpy as np
from jax import lax
from jax.experimental import pallas as pl
from jax.experimental.pallas import tpu as pltpu
from jax.sharding import PartitionSpec as P

MESH = pl.DeviceIdType.MESH


def field_product(first, second):
    return (
        (first[0] * second[0] + 2 * first[1] * second[1]) % 5,
        (first[0] * second[1] + first[1] * second[0]) % 5,
    )


def paley_table():
    elements = [(alpha, beta) for alpha in range(5) for beta in range(5)]
    squares = set()
    for item in elements:
        if item != (0, 0):
            squares.add(field_product(item, item))
    jacobi = np.zeros((25, 25))
    for left in range(25):
        for right in range(25):
            diff = (
                (elements[left][0] - elements[right][0]) % 5,
                (elements[left][1] - elements[right][1]) % 5,
            )
            if diff == (0, 0):
                jacobi[left, right] = 0.0
            elif diff in squares:
                jacobi[left, right] = 1.0
            else:
                jacobi[left, right] = -1.0
    conference = np.zeros((26, 26))
    conference[0, 1:] = 1.0
    conference[1:, 0] = 1.0
    conference[1:, 1:] = jacobi
    return np.kron(conference, np.array([[1.0, -1.0], [-1.0, -1.0]])) + np.kron(
        np.eye(26), np.array([[1.0, 1.0], [1.0, -1.0]])
    )


def sylvester_table(order):
    table = np.ones((1, 1))
    while table.shape[0] < order:
        table = np.kron(table, np.array([[1.0, 1.0], [1.0, -1.0]]))
    return table


def activate(sums, gate_scale, up_scale, width):
    gate = sums[:, :width] * gate_scale
    up_val = sums[:, width:] * up_scale
    return (jax.nn.silu(gate) * up_val).astype(jnp.bfloat16)


def on_device(
    act_codes, act_exps, gate_codes, up_codes, down_codes, gate_scale, up_scale, down_scale
):
    row_count, col_count = act_codes.shape
    blocks = act_exps.shape[1]
    scales = jnp.exp2(act_exps.astype(jnp.float32))
    features = (
        (
            act_codes.reshape(row_count, blocks, col_count // blocks).astype(jnp.float32)
            * scales[:, :, None]
        )
        .reshape(row_count, col_count)
        .astype(jnp.bfloat16)
    )
    width = gate_codes.shape[1]
    piece = lax.all_gather(features, "ffn", axis=0, tiled=True)
    gate_part = jnp.dot(piece, gate_codes, preferred_element_type=jnp.float32)
    up_part = jnp.dot(piece, up_codes, preferred_element_type=jnp.float32)
    partial_sums = jnp.concatenate([gate_part, up_part], axis=1)
    summed = lax.psum(partial_sums, "hid")
    hidden = activate(summed, gate_scale, up_scale, width)
    parts = lax.axis_size("ffn")
    tokens = hidden.shape[0]
    per_dev = tokens // parts
    local = width // 52
    small_table = jnp.asarray(paley_table(), dtype=jnp.bfloat16)
    outer_table = jnp.asarray(sylvester_table(parts), dtype=jnp.float32)
    inner_table = jnp.asarray(sylvester_table(local), dtype=jnp.float32)
    norm_factor = 1.0 / np.sqrt(parts * width)
    grouped = hidden.reshape(parts, per_dev, width)
    block = lax.all_to_all(grouped, "ffn", split_axis=0, concat_axis=0, tiled=True)
    items = block.shape[1]
    cube = block.reshape(parts, items, local, 52)
    mixed = jnp.einsum("snli,ik->snlk", cube, small_table, preferred_element_type=jnp.float32)
    across = jnp.einsum("snlk,sS->Snlk", mixed, outer_table, precision=lax.Precision.HIGHEST)
    turned = jnp.einsum("Snlk,lL->SnLk", across, inner_table, precision=lax.Precision.HIGHEST)
    rotated = (turned * norm_factor).reshape(parts, items, width).astype(jnp.bfloat16)
    returned = lax.all_to_all(rotated, "ffn", split_axis=0, concat_axis=0, tiled=True)
    rotated_rows = returned.reshape(tokens, width)
    total = lax.psum_scatter(
        jnp.dot(rotated_rows, down_codes, preferred_element_type=jnp.float32),
        "ffn",
        scatter_dimension=0,
        tiled=True,
    )
    return (total * down_scale).astype(jnp.bfloat16)


LANES = 128
ORDER = 52
SPLIT = 4
TILE_ROWS = 256
GROUPS = 2
RING = 12
PAD = 24
FULL = 32


def flip(index, mask):
    if mask == 1:
        return index + 1 - 2 * (index % 2)
    if mask == 2:
        return (index + 2) % 4
    if mask == 3:
        return 3 - index
    return index


def sign_of(first, second):
    low = (first % 2) * (second % 2)
    high = (first // 2) * (second // 2)
    odd = (low + high) % 2
    return jnp.asarray(1 - 2 * odd, jnp.int32).astype(jnp.float32)


def cut_chunk(blocks):
    cuts = []
    while blocks > 5:
        cuts.append(4)
        blocks -= 4
    if blocks > 2:
        cuts += [blocks - 2, 2]
    else:
        cuts.append(blocks)
    return cuts


def layer_kernel(plan, *refs):
    rows, depth, width, feats, norm = plan
    chunk = width // SPLIT
    cuts = [blocks * LANES for blocks in cut_chunk(chunk // LANES)]
    starts = [sum(cuts[:index]) for index in range(len(cuts))]
    count = len(cuts)
    blocks = depth // LANES
    half = width // GROUPS
    down_tiles = half // TILE_ROWS
    refs = list(refs)
    (codes, exps, gate_hbm, up_hbm, down_hbm, scales, dscale, table_hbm, out) = refs[:9]
    (table, down, fold, xrecv, xfull, xmat, zsum, zpair, zall, rot, part, obuf, orecv) = refs[9:22]
    weights, own, psend, precv, xsend, xgot, hall = [refs[22 + count * k : 22 + count * (k + 1)] for k in range(7)]
    (unit_sem, table_sem, down_sem, fs, fr, ps, pr, cs, cr, hs, hr, ys, yr, zs, zr, os, orr) = refs[22 + 7 * count :]
    me_g = lax.axis_index("groups")
    me_f = lax.axis_index("ffn")
    me_h = lax.axis_index("hid")
    me_x, me_c = me_h // 2, me_h % 2
    others = [(across, mask) for across in (1, 0) for mask in (3, 2, 1, 0) if across or mask]

    def token_peer(across, mask):
        return {"groups": (me_g + across) % 2, "ffn": flip(me_f, mask)}

    units = [(sub, other, which) for sub in range(count) for other in (1, 0) for which in (0, 1)]

    def unit_copy(index):
        sub, other, which = units[index]
        source = up_hbm if which else gate_hbm
        at = pl.multiple_of((2 * me_g + (me_c + other) % 2) * chunk + starts[sub], LANES)
        return pltpu.make_async_copy(
            source.at[:, pl.ds(at, cuts[sub])], weights[sub].at[2 * other + which], unit_sem.at[index]
        )

    def down_copy(index):
        at = pl.multiple_of(me_g * half + index * TILE_ROWS, TILE_ROWS)
        return pltpu.make_async_copy(
            down_hbm.at[pl.ds(at, TILE_ROWS), :], down.at[pl.ds(index * TILE_ROWS, TILE_ROWS), :], down_sem.at[index]
        )

    def table_copy(sub):
        piece = pl.ds(starts[sub], cuts[sub])
        return pltpu.make_async_copy(table_hbm.at[piece, :], table.at[piece, :], table_sem.at[sub])

    for index in range(min(RING, len(units))):
        unit_copy(index).start()
    for sub in range(count):
        table_copy(sub).start()

    barrier = pltpu.get_barrier_semaphore()
    for across, mask in others:
        pl.semaphore_signal(barrier, inc=1, device_id=token_peer(across, mask), device_id_type=MESH)
    for mask in (1, 2, 3):
        pl.semaphore_signal(barrier, inc=1, device_id={"hid": flip(me_h, mask)}, device_id_type=MESH)

    powers = lax.shift_left(jnp.ones_like(exps[...]), exps[...] + 10).astype(jnp.float32) * (2.0**-10)
    for block in range(blocks):
        at = block * LANES
        scale = powers[:, at // feats : at // feats + 1]
        fold[0, pl.ds(block * rows, rows), :] = codes[:, pl.ds(at, LANES)].astype(jnp.float32) * scale
    xrecv[0] = fold[0].astype(jnp.bfloat16)
    pl.semaphore_wait(barrier, 10)

    def feat_copy(across, mask):
        slot = 4 * across + mask
        return pltpu.make_async_remote_copy(
            src_ref=xrecv.at[0], dst_ref=xrecv.at[slot], send_sem=fs.at[slot - 1], recv_sem=fr.at[slot - 1],
            device_id=token_peer(across, mask), device_id_type=MESH,
        )

    for across, mask in others:
        feat_copy(across, mask).start()
    xfull[...] = jnp.zeros_like(xfull)
    for across, mask in others:
        feat_copy(across, mask).wait_recv()
    for across in range(2):
        for mask in range(4):
            fold[((me_g + across) % 2) * 4 + flip(me_f, mask)] = xrecv[4 * across + mask].astype(jnp.float32)
    for owner in range(2 * SPLIT):
        at = (owner // SPLIT) * PAD + (owner % SPLIT) * rows
        for block in range(blocks):
            xfull[pl.ds(at, rows), pl.ds(block * LANES, LANES)] = fold[owner, pl.ds(block * rows, rows), :]
    xmat[...] = xfull[...].astype(jnp.bfloat16)

    def core_copy(sub):
        return pltpu.make_async_remote_copy(
            src_ref=psend[sub], dst_ref=precv[sub], send_sem=ps.at[sub], recv_sem=pr.at[sub],
            device_id={"hid": flip(me_h, 1)}, device_id_type=MESH,
        )

    def chip_copy(sub):
        return pltpu.make_async_remote_copy(
            src_ref=xsend[sub], dst_ref=xgot[sub], send_sem=cs.at[sub], recv_sem=cr.at[sub],
            device_id={"hid": flip(me_h, 2)}, device_id_type=MESH,
        )

    def hidden_copy(sub, mask):
        return pltpu.make_async_remote_copy(
            src_ref=hall[sub].at[0], dst_ref=hall[sub].at[mask],
            send_sem=hs.at[sub * 3 + mask - 1], recv_sem=hr.at[sub * 3 + mask - 1],
            device_id={"ffn": flip(me_f, mask)}, device_id_type=MESH,
        )

    def pair_copy():
        return pltpu.make_async_remote_copy(
            src_ref=zpair.at[0], dst_ref=zpair.at[1], send_sem=ys.at[0], recv_sem=yr.at[0],
            device_id={"groups": 1 - me_g}, device_id_type=MESH,
        )

    def z_copy(mask):
        return pltpu.make_async_remote_copy(
            src_ref=zall.at[0], dst_ref=zall.at[mask], send_sem=zs.at[mask - 1], recv_sem=zr.at[mask - 1],
            device_id={"hid": flip(me_h, mask)}, device_id_type=MESH,
        )

    def out_copy(across, mask):
        slot = 4 * across + mask - 1
        return pltpu.make_async_remote_copy(
            src_ref=obuf.at[((me_x + me_g + across) % 2) * 4 + flip(me_f, mask)], dst_ref=orecv.at[slot],
            send_sem=os.at[slot], recv_sem=orr.at[slot],
            device_id=token_peer(across, mask), device_id_type=MESH,
        )

    def sum_cores(sub):
        core_copy(sub).wait_recv()
        for which in range(2):
            xsend[sub][which] = own[sub][which, 1 - me_x] + precv[sub][which, 1 - me_x]
        chip_copy(sub).start()

    def finish_hidden(sub):
        chip_copy(sub).wait_recv()
        piece = pl.ds(starts[sub], cuts[sub])
        sums = [own[sub][which, me_x] + precv[sub][which, me_x] + xgot[sub][which] for which in range(2)]
        gate = sums[0] * scales[0:1, piece]
        value = gate / (1.0 + jnp.exp(-gate)) * (sums[1] * scales[1:2, piece])
        padded = jnp.concatenate([value, jnp.zeros((FULL - PAD, cuts[sub]), jnp.float32)], axis=0)
        hall[sub][0] = padded.astype(jnp.bfloat16)
        for mask in (3, 2, 1):
            hidden_copy(sub, mask).start()

    def mix(sub):
        table_copy(sub).wait()
        total = hall[sub][0].astype(jnp.float32) * sign_of(me_f, me_f)
        for mask in (1, 2, 3):
            hidden_copy(sub, mask).wait_recv()
            total = total + hall[sub][mask].astype(jnp.float32) * sign_of(flip(me_f, mask), me_f)
        total = total[:PAD]
        high = total.astype(jnp.bfloat16).astype(jnp.float32)
        both = jnp.concatenate([high, total - high], axis=0).astype(jnp.bfloat16)
        mixed = jnp.dot(both, table[pl.ds(starts[sub], cuts[sub]), :], preferred_element_type=jnp.float32)
        mixed = mixed[:PAD] + mixed[PAD:]
        if sub == 0:
            zsum[...] = mixed
        else:
            zsum[...] += mixed

    down_next = 0
    for index, (sub, other, which) in enumerate(units):
        unit_copy(index).wait()
        value = jnp.dot(xmat[...], weights[sub][2 * other + which], preferred_element_type=jnp.float32)
        target = psend[sub] if other else own[sub]
        for group in range(2):
            target[which, group] = value[group * PAD : (group + 1) * PAD]
        if index + RING < len(units):
            unit_copy(index + RING).start()
        elif down_next < down_tiles:
            down_copy(down_next).start()
            down_next += 1
        if which == 1:
            if other:
                core_copy(sub).start()
                if sub >= 1:
                    finish_hidden(sub - 1)
            else:
                sum_cores(sub)
                if sub >= 1:
                    mix(sub - 1)
    while down_next < down_tiles:
        down_copy(down_next).start()
        down_next += 1
    finish_hidden(count - 1)
    mix(count - 1)

    spare = jnp.zeros((FULL - PAD, chunk), jnp.float32)
    zpair[0] = jnp.concatenate([zsum[...], spare], axis=0).astype(jnp.bfloat16)
    pair_copy().start()
    mine = zsum[...] * sign_of(me_g, me_g)
    pair_copy().wait_recv()
    mine = mine + zpair[1].astype(jnp.float32)[:PAD]
    zall[0] = jnp.concatenate([mine, spare], axis=0).astype(jnp.bfloat16)
    for mask in (3, 2, 1):
        z_copy(mask).start()
    for index in range(down_tiles):
        down_copy(index).wait()
    for mask in (1, 2, 3):
        z_copy(mask).wait_recv()
    for target in range(2):
        groups = []
        for far in range(2):
            total = zall[2 * far].astype(jnp.float32) * (sign_of(me_c, target) * norm)
            total = total + zall[2 * far + 1].astype(jnp.float32) * (sign_of(1 - me_c, target) * norm)
            groups.append(total[:PAD])
        rot[target] = jnp.concatenate(groups, axis=0).astype(jnp.bfloat16)

    @pl.loop(0, depth // 512)
    def _(tile):
        at = pl.ds(pl.multiple_of(tile * 512, 512), 512)
        total = jnp.zeros((2 * PAD, 512), jnp.float32)
        for target in range(2):
            total = total + jnp.dot(
                rot[target], down[pl.ds(target * chunk, chunk), at], preferred_element_type=jnp.float32
            )
        part[:, at] = total

    for owner in range(2 * SPLIT):
        at = (owner // SPLIT) * PAD + (owner % SPLIT) * rows
        for block in range(blocks):
            fold[owner, pl.ds(block * rows, rows), :] = part[pl.ds(at, rows), pl.ds(block * LANES, LANES)]
    obuf[...] = fold[...].astype(jnp.bfloat16)
    for across, mask in others:
        out_copy(across, mask).start()
    total = fold[((me_x + me_g) % 2) * 4 + me_f]
    for across, mask in others:
        out_copy(across, mask).wait_recv()
        total = total + orecv[4 * across + mask - 1].astype(jnp.float32)
    fold[0] = total
    for block in range(blocks):
        at = pl.ds(block * LANES, LANES)
        out[:, at] = (fold[0, pl.ds(block * rows, rows), :] * dscale[:, at]).astype(jnp.bfloat16)

    for across, mask in others:
        feat_copy(across, mask).wait_send()
        out_copy(across, mask).wait_send()
    pair_copy().wait_send()
    for mask in (1, 2, 3):
        z_copy(mask).wait_send()
        for sub in range(count):
            hidden_copy(sub, mask).wait_send()
    for sub in range(count):
        core_copy(sub).wait_send()
        chip_copy(sub).wait_send()


def fused_on_device(
    act_codes, act_exps, gate_codes, up_codes, down_codes, gate_scale, up_scale, down_scale
):
    rows, depth = act_codes.shape
    width = gate_codes.shape[1]
    chunk = width // SPLIT
    feats = depth // act_exps.shape[1]
    cuts = [blocks * LANES for blocks in cut_chunk(chunk // LANES)]
    count = len(cuts)
    norm = float(1.0 / np.sqrt(width * lax.axis_size("ffn")))
    table = jnp.asarray(
        np.kron(sylvester_table(chunk // ORDER), paley_table()).astype(np.float32), dtype=jnp.bfloat16
    )
    folded = rows * (depth // LANES)
    vmem = pl.BlockSpec(memory_space=pltpu.VMEM)
    hbm = pl.BlockSpec(memory_space=pl.ANY)
    f32, bf16 = jnp.float32, jnp.bfloat16
    half = width // GROUPS
    scratch = [
        pltpu.VMEM((chunk, chunk), bf16),
        pltpu.VMEM((half, depth), bf16),
        pltpu.VMEM((2 * SPLIT, folded, LANES), f32),
        pltpu.VMEM((2 * SPLIT, folded, LANES), bf16),
        pltpu.VMEM((2 * PAD, depth), f32),
        pltpu.VMEM((2 * PAD, depth), bf16),
        pltpu.VMEM((PAD, chunk), f32),
        pltpu.VMEM((2, FULL, chunk), bf16),
        pltpu.VMEM((SPLIT, FULL, chunk), bf16),
        pltpu.VMEM((2, 2 * PAD, chunk), bf16),
        pltpu.VMEM((2 * PAD, depth), f32),
        pltpu.VMEM((2 * SPLIT, folded, LANES), bf16),
        pltpu.VMEM((2 * SPLIT - 1, folded, LANES), bf16),
    ]
    scratch += [pltpu.VMEM((4, depth, cut), bf16) for cut in cuts]
    for _ in range(3):
        scratch += [pltpu.VMEM((2, 2, PAD, cut), f32) for cut in cuts]
    for _ in range(2):
        scratch += [pltpu.VMEM((2, PAD, cut), f32) for cut in cuts]
    scratch += [pltpu.VMEM((SPLIT, FULL, cut), bf16) for cut in cuts]
    dma = pltpu.SemaphoreType.DMA
    scratch += [dma((4 * count,)), dma((count,)), dma((half // TILE_ROWS,)), dma((7,)), dma((7,))]
    scratch += [dma((count,)) for _ in range(4)]
    scratch += [dma((3 * count,)) for _ in range(2)]
    scratch += [dma((1,)), dma((1,)), dma((3,)), dma((3,)), dma((7,)), dma((7,))]
    at = (2 * lax.axis_index("groups") + lax.axis_index("hid") % 2) * chunk
    scales = jnp.stack([lax.dynamic_slice(each, (at,), (chunk,)) for each in (gate_scale, up_scale)])
    return pl.pallas_call(
        functools.partial(layer_kernel, (rows, depth, width, feats, norm)),
        out_shape=jax.ShapeDtypeStruct((rows, depth), bf16),
        in_specs=[vmem, vmem, hbm, hbm, hbm, vmem, vmem, hbm],
        out_specs=vmem,
        scratch_shapes=scratch,
        compiler_params=pltpu.CompilerParams(
            collective_id=0, has_side_effects=True, vmem_limit_bytes=62 * 2**20
        ),
        cost_estimate=pl.CostEstimate(
            flops=6 * rows * SPLIT * depth * width, bytes_accessed=3 * depth * width, transcendentals=0
        ),
    )(
        act_codes, act_exps, gate_codes, up_codes, down_codes,
        scales, down_scale.reshape(1, depth), table,
    )


def solution(mesh):
    in_specs = (
        P(("groups", "ffn"), "hid"),
        P(("groups", "ffn"), "hid"),
        P("hid", "ffn"),
        P("hid", "ffn"),
        P("ffn", "hid"),
        P("ffn"),
        P("ffn"),
        P("hid"),
    )
    out_specs = P(("groups", "ffn"), "hid")
    square = mesh.shape["groups"] == GROUPS and mesh.shape["ffn"] == SPLIT and mesh.shape["hid"] == SPLIT
    return jax.shard_map(
        fused_on_device if square else on_device, mesh=mesh, in_specs=in_specs, out_specs=out_specs, check_vma=False
    )
```

time: 57 us -> 59 us (1.035)
  Pallas kernels: 52.5 us -> 55.1 us
  local copies, waits for them, and re-layouts: 4.11 us -> 2.95 us
  other arithmetic: 0 us -> 0.62 us
    reshape x2 -> x0, local copies, waits for them, and re-layouts: 2.74 us -> none  [the longest x1 1.37 us: fused_on_device(): gate_scale.reshape(1, width)]
    pallas_call x1, Pallas kernels: 52.5 us -> 55.1 us  [fused_on_device(): pl.pallas_call(functools.partial(layer_kernel, (rows, depth, width, feats...]
    dynamic_slice x0 -> x2, local copies, waits for them, and re-layouts: none -> 1.56 us  [fused_on_device(): lax.dynamic_slice(each, (at,), (chunk,))]
    another operation x0 -> x1, other arithmetic: none -> 0.62 us  [fused_on_device(): jnp.stack([lax.dynamic_slice(each, (at,), (chunk,)) for each in (gate_sca...]
where the time goes in v2:
time: 59 us; the launch traced here: 58.7 us
  Pallas kernels  55.1 us (93%)
  local copies, waits for them, and re-layouts  2.95 us (5%)
  other arithmetic  0.62 us (1%)
    pallas_call x1, Pallas kernels, fused_on_device(): pl.pallas_call(functools.partial(layer_kernel, (rows, depth, width, feats...  55.1 us
    dynamic_slice x2, local copies, waits for them, and re-layouts, fused_on_device(): lax.dynamic_slice(each, (at,), (chunk,))  1.56 us
    unnamed x1, local copies, waits for them, and re-layouts  1.38 us

profile of v2, /device:TPU:0, one launch (start us, length us, event | category | flops | bytes accessed | tf_op | source)
XLA Modules:
  0.0 58.7 jit_solution(5124879309252438031)
XLA Ops:
  0.0 0.8 %dynamic_slice.6 = f32[1664]{0:T(1024)S(1)} dynamic-slice(f32[6656]{0:T(1024)} %param.14, s32[]{:T(128)S(6)} %select_n.12), dynamic_slice_sizes={1664} | dynamic-slice | bytes 13316 | tf_op jit(solution)/shard_map/dynamic_slice | solution.py:436
  0.8 0.8 %dynamic_slice.7 = f32[1664]{0:T(1024)S(1)} dynamic-slice(f32[6656]{0:T(1024)} %param.15, s32[]{:T(128)S(6)} %select_n.12), dynamic_slice_sizes={1664} | dynamic-slice | bytes 13316 | tf_op jit(solution)/shard_map/dynamic_slice | solution.py:436
  1.6 0.6 %pad_maximum_fusion.refs_5_ = f32[2,1664]{1,0:T(2,128)} fusion(f32[1,1664]{1,0:T(1,128)S(1)} %stack.10, f32[1,1664]{1,0:T(1,128)S(1)} %stack.9), kind=kLoop, calls=%fused_computation | loop fusion | flops 3328 | bytes 26624 | tf_op jit(solution)/shard_map/stack | solution.py:436
  2.2 55.1 %shard_map.91 = bf16[5,2048]{1,0:T(8,128)(2,1)} custom-call(s32[5,2048]{1,0:T(8,128)} %refs_0_.1, s32[5,16]{1,0:T(8,128)} %refs_1_.1, bf16[2048,6656]{1,0:T(8,128)(2,1)} %refs_2_.1, bf16[2048,6656]{1,0:T(8,128)(2,1)} %refs_3_.1, bf16[6656,2048]{1,0:T(8,128)(2,1)} %refs_4_.1, f32[2,1664]{1,0:T(2,128)} %pad_maximum_fusion.refs_5_, f32[1,2048]{1,0:T(1,128)} %bitcast.1, ...), custom_call_target="tpu_custom_call" | custom-call | flops 1635778560 | bytes 40894464 | tf_op jit(solution)/shard_map/pallas_call | solution.py:437
  57.3 1.4 %copy.11 = bf16[5,2048]{1,0:T(8,128)(2,1)} copy(bf16[5,2048]{1,0:T(8,128)(2,1)} %shard_map.91) | data formatting | bytes 40960
  (2 shorter events, 0.0 us)

commit v3 on v2

--- a/solution.py
+++ b/solution.py
@@ -156,10 +156,10 @@
     half = width // GROUPS
     down_tiles = half // TILE_ROWS
     refs = list(refs)
-    (codes, exps, gate_hbm, up_hbm, down_hbm, scales, dscale, table_hbm, out) = refs[:9]
-    (table, down, fold, xrecv, xfull, xmat, zsum, zpair, zall, rot, part, obuf, orecv) = refs[9:22]
-    weights, own, psend, precv, xsend, xgot, hall = [refs[22 + count * k : 22 + count * (k + 1)] for k in range(7)]
-    (unit_sem, table_sem, down_sem, fs, fr, ps, pr, cs, cr, hs, hr, ys, yr, zs, zr, os, orr) = refs[22 + 7 * count :]
+    (codes, exps, gate_hbm, up_hbm, down_hbm, gscale, uscale, dscale, table_hbm, out) = refs[:10]
+    (table, down, fold, xrecv, xfull, xmat, zsum, zpair, zall, rot, part, obuf, orecv) = refs[10:23]
+    weights, own, psend, precv, xsend, xgot, hall = [refs[23 + count * k : 23 + count * (k + 1)] for k in range(7)]
+    (unit_sem, table_sem, down_sem, fs, fr, ps, pr, cs, cr, hs, hr, ys, yr, zs, zr, os, orr) = refs[23 + 7 * count :]
     me_g = lax.axis_index("groups")
     me_f = lax.axis_index("ffn")
     me_h = lax.axis_index("hid")
@@ -248,15 +248,21 @@
             device_id={"ffn": flip(me_f, mask)}, device_id_type=MESH,
         )
 
-    def pair_copy():
-        return pltpu.make_async_remote_copy(
-            src_ref=zpair.at[0], dst_ref=zpair.at[1], send_sem=ys.at[0], recv_sem=yr.at[0],
+    first = (chunk // LANES + 1) // 2 * LANES
+    sides = ((0, first), (first, chunk - first))
+
+    def pair_copy(side):
+        piece = pl.ds(*sides[side])
+        return pltpu.make_async_remote_copy(
+            src_ref=zpair.at[0, :, piece], dst_ref=zpair.at[1, :, piece], send_sem=ys.at[side], recv_sem=yr.at[side],
             device_id={"groups": 1 - me_g}, device_id_type=MESH,
         )
 
-    def z_copy(mask):
-        return pltpu.make_async_remote_copy(
-            src_ref=zall.at[0], dst_ref=zall.at[mask], send_sem=zs.at[mask - 1], recv_sem=zr.at[mask - 1],
+    def z_copy(side, mask):
+        piece = pl.ds(*sides[side])
+        slot = 3 * side + mask - 1
+        return pltpu.make_async_remote_copy(
+            src_ref=zall.at[0, :, piece], dst_ref=zall.at[mask, :, piece], send_sem=zs.at[slot], recv_sem=zr.at[slot],
             device_id={"hid": flip(me_h, mask)}, device_id_type=MESH,
         )
 
@@ -276,10 +282,14 @@
 
     def finish_hidden(sub):
         chip_copy(sub).wait_recv()
-        piece = pl.ds(starts[sub], cuts[sub])
+        at = pl.multiple_of((2 * me_g + me_c) * chunk + starts[sub], LANES)
+
+        def column(ref):
+            return ref[pl.ds(at, cuts[sub])].reshape(1, cuts[sub])
+
         sums = [own[sub][which, me_x] + precv[sub][which, me_x] + xgot[sub][which] for which in range(2)]
-        gate = sums[0] * scales[0:1, piece]
-        value = gate / (1.0 + jnp.exp(-gate)) * (sums[1] * scales[1:2, piece])
+        gate = sums[0] * column(gscale)
+        value = gate / (1.0 + jnp.exp(-gate)) * (sums[1] * column(uscale))
         padded = jnp.concatenate([value, jnp.zeros((FULL - PAD, cuts[sub]), jnp.float32)], axis=0)
         hall[sub][0] = padded.astype(jnp.bfloat16)
         for mask in (3, 2, 1):
@@ -328,19 +338,24 @@
     finish_hidden(count - 1)
     mix(count - 1)
 
-    spare = jnp.zeros((FULL - PAD, chunk), jnp.float32)
-    zpair[0] = jnp.concatenate([zsum[...], spare], axis=0).astype(jnp.bfloat16)
-    pair_copy().start()
-    mine = zsum[...] * sign_of(me_g, me_g)
-    pair_copy().wait_recv()
-    mine = mine + zpair[1].astype(jnp.float32)[:PAD]
-    zall[0] = jnp.concatenate([mine, spare], axis=0).astype(jnp.bfloat16)
-    for mask in (3, 2, 1):
-        z_copy(mask).start()
+    for side, (at, wide) in enumerate(sides):
+        spare = jnp.zeros((FULL - PAD, wide), jnp.float32)
+        piece = pl.ds(at, wide)
+        zpair[0, :, piece] = jnp.concatenate([zsum[:, piece], spare], axis=0).astype(jnp.bfloat16)
+        pair_copy(side).start()
+    for side, (at, wide) in enumerate(sides):
+        spare = jnp.zeros((FULL - PAD, wide), jnp.float32)
+        piece = pl.ds(at, wide)
+        pair_copy(side).wait_recv()
+        mine = zsum[:, piece] * sign_of(me_g, me_g) + zpair[1, :, piece].astype(jnp.float32)[:PAD]
+        zall[0, :, piece] = jnp.concatenate([mine, spare], axis=0).astype(jnp.bfloat16)
+        for mask in (3, 2, 1):
+            z_copy(side, mask).start()
     for index in range(down_tiles):
         down_copy(index).wait()
-    for mask in (1, 2, 3):
-        z_copy(mask).wait_recv()
+    for side in range(2):
+        for mask in (1, 2, 3):
+            z_copy(side, mask).wait_recv()
     for target in range(2):
         groups = []
         for far in range(2):
@@ -378,9 +393,11 @@
     for across, mask in others:
         feat_copy(across, mask).wait_send()
         out_copy(across, mask).wait_send()
-    pair_copy().wait_send()
+    for side in range(2):
+        pair_copy(side).wait_send()
+        for mask in (1, 2, 3):
+            z_copy(side, mask).wait_send()
     for mask in (1, 2, 3):
-        z_copy(mask).wait_send()
         for sub in range(count):
             hidden_copy(sub, mask).wait_send()
     for sub in range(count):
@@ -431,13 +448,11 @@
     scratch += [dma((4 * count,)), dma((count,)), dma((half // TILE_ROWS,)), dma((7,)), dma((7,))]
     scratch += [dma((count,)) for _ in range(4)]
     scratch += [dma((3 * count,)) for _ in range(2)]
-    scratch += [dma((1,)), dma((1,)), dma((3,)), dma((3,)), dma((7,)), dma((7,))]
-    at = (2 * lax.axis_index("groups") + lax.axis_index("hid") % 2) * chunk
-    scales = jnp.stack([lax.dynamic_slice(each, (at,), (chunk,)) for each in (gate_scale, up_scale)])
+    scratch += [dma((2,)), dma((2,)), dma((6,)), dma((6,)), dma((7,)), dma((7,))]
     return pl.pallas_call(
         functools.partial(layer_kernel, (rows, depth, width, feats, norm)),
         out_shape=jax.ShapeDtypeStruct((rows, depth), bf16),
-        in_specs=[vmem, vmem, hbm, hbm, hbm, vmem, vmem, hbm],
+        in_specs=[vmem, vmem, hbm, hbm, hbm, vmem, vmem, vmem, hbm],
         out_specs=vmem,
         scratch_shapes=scratch,
         compiler_params=pltpu.CompilerParams(
@@ -448,7 +463,7 @@
         ),
     )(
         act_codes, act_exps, gate_codes, up_codes, down_codes,
-        scales, down_scale.reshape(1, depth), table,
+        gate_scale, up_scale, down_scale.reshape(1, depth), table,
     )
 
 

time: 59 us -> 56.7 us (0.961)
  local copies, waits for them, and re-layouts: 2.95 us -> 1.38 us
  other arithmetic: 0.62 us -> 0 us
    dynamic_slice x2 -> x0, local copies, waits for them, and re-layouts: 1.56 us -> none  [fused_on_device(): lax.dynamic_slice(each, (at,), (chunk,))]
    another operation x1 -> x0, other arithmetic: 0.62 us -> none  [fused_on_device(): jnp.stack([lax.dynamic_slice(each, (at,), (chunk,)) for each in (gate_sca...]
where the time goes in v3:
time: 56.7 us; the launch traced here: 56.4 us
  Pallas kernels  55 us (97%)
  local copies, waits for them, and re-layouts  1.38 us (2%)
    pallas_call x1, Pallas kernels, fused_on_device(): pl.pallas_call(functools.partial(layer_kernel, (rows, depth, width, feats...  55 us
    unnamed x1, local copies, waits for them, and re-layouts  1.38 us

profile of v3, /device:TPU:0, one launch (start us, length us, event | category | flops | bytes accessed | tf_op | source)
XLA Modules:
  0.0 56.4 jit_solution(10181674813345087900)
XLA Ops:
  0.0 55.0 %shard_map.91 = bf16[5,2048]{1,0:T(8,128)(2,1)} custom-call(s32[5,2048]{1,0:T(8,128)} %refs_0_.1, s32[5,16]{1,0:T(8,128)} %refs_1_.1, bf16[2048,6656]{1,0:T(8,128)(2,1)} %refs_2_.1, bf16[2048,6656]{1,0:T(8,128)(2,1)} %refs_3_.1, bf16[6656,2048]{1,0:T(8,128)(2,1)} %refs_4_.1, f32[6656]{0:T(1024)} %refs_5_.1, f32[6656]{0:T(1024)} %refs_6_.1, ...), custom_call_target="tpu_custom_call" | custom-call | flops 1635778560 | bytes 40894464 | tf_op jit(solution)/shard_map/pallas_call | solution.py:452
  55.1 1.4 %copy.11 = bf16[5,2048]{1,0:T(8,128)(2,1)} copy(bf16[5,2048]{1,0:T(8,128)(2,1)} %shard_map.91) | data formatting | bytes 40960
